TPU v7x, 128 devices: a whole 4x4x4 slice. The times are simulated.
128 devices in a mesh: section: 2 (over x_hi), tensor: 4 (over z), dp: 16 (over y, x_lo, core).
Axes of the slice: x: 4 (x_hi: 2, x_lo: 2; x = x_hi * 2 + x_lo), y: 4, z: 4, core: 2. Of those that a mesh axis runs over, the one named last changes fastest.
Arguments:
- embedded: bfloat16 [8192, 768], P('dp'), may hold values from -6 to 6
- expert_index: int32 [2, 8192, 1], P('section', 'dp'), may hold values from 0 to 1
- buckets: int32 [128, 128], replicated, may hold values from 0 to 31
- rel_bias: float32 [32, 12], P(None, 'tensor'), may hold values from -6 to 6
- gain_attn: float32 [2, 768], P('section'), may hold values from 0.5 to 1.5
- w_qkv: bfloat16 [2, 3, 768, 768], P('section', None, None, 'tensor'), may hold values from -0.21875 to 0.21875
- w_out: bfloat16 [2, 768, 768], P('section', 'tensor'), may hold values from -1.25 to 1.25
- gain_ffn: float32 [2, 768], P('section'), may hold values from 0.5 to 1.5
- w_router: bfloat16 [2, 768, 2], P('section'), may hold values from -0.15625 to 0.15625
- w_in: bfloat16 [2, 2, 768, 3072], P('section', None, None, 'tensor'), may hold values from -0.21875 to 0.21875
- w_down: bfloat16 [2, 2, 3072, 768], P('section', None, 'tensor'), may hold values from -0.21875 to 0.21875
- cotangent: bfloat16 [8192, 768], P('dp'), may hold values from -6 to 6
Outputs:
- hidden: float32 [2, 8192, 768], P('section', 'dp')
- grad_input: float32 [2, 8192, 768], P('section', 'dp')
- grad_rel_bias: float32 [32, 12], P(None, 'tensor')
- grad_gain_attn: float32 [2, 768], P('section')
- grad_qkv: float32 [2, 3, 768, 768], P('section', None, None, 'tensor')
- grad_out: float32 [2, 768, 768], P('section', 'tensor')
- grad_gain_ffn: float32 [2, 768], P('section')
- grad_router: float32 [2, 768, 2], P('section')
- grad_in: float32 [2, 2, 768, 3072], P('section', None, None, 'tensor')
- grad_down: float32 [2, 2, 3072, 768], P('section', None, 'tensor')
Inputs may be any that keep to these rules, and one draw needn't show every extreme that they name: `expert_index`: each token's expert in each layer; every one of the 2 experts is chosen by some token. `buckets`: bucket of each pair of query and key positions within a sequence.
All inputs are finite; a program needn't handle non-finite values.
Results may differ from a plain program's by a relative error of at most 0.034.
Values may be sent and summed in bfloat16 or wider, within the bound.
A program may use at most 128 MiB of HBM per device.

v0:
```python
import jax
import jax.numpy as jnp
from jax import lax
from jax.sharding import PartitionSpec as P

MB = 2


eps_norm = 1e-06
score_scale = 0.125
exact_mode = lax.Precision.HIGHEST


def from_behind(x, axis, by):
    count = lax.axis_size(axis)
    pairs = [(i, i + by) for i in range(count) if 0 <= i + by < count]
    return lax.ppermute(x, axis, pairs)


def rms_apply(values, gain_vec):
    return (
        values * lax.rsqrt(jnp.mean(values * values, axis=-1, keepdims=True) + eps_norm) * gain_vec
    )


def route_gate(normed_wide, router_wide, choose):
    logits = jnp.dot(normed_wide, router_wide, precision=exact_mode)
    shifted = logits - jnp.max(logits, axis=-1, keepdims=True)
    powers = jnp.exp(shifted)
    return jnp.sum(
        powers / jnp.sum(powers, axis=-1, keepdims=True) * choose, axis=-1, keepdims=True
    )


def attend_scores(hidden, gain_attn, w_qkv, position_bias, seq_len):
    normed = rms_apply(hidden, gain_attn).astype(jnp.bfloat16)
    projected = jnp.einsum("rd,kdc->krc", normed, w_qkv, preferred_element_type=jnp.float32).astype(
        jnp.bfloat16
    )
    head_count = position_bias.shape[0]
    row_count, local_width = (projected.shape[1], projected.shape[2])
    split_heads = projected.reshape(
        3, row_count // seq_len, seq_len, head_count, local_width // head_count
    )
    scores = (
        jnp.einsum(
            "bihc,bjhc->bhij", split_heads[0], split_heads[1], preferred_element_type=jnp.float32
        )
        * score_scale
        + position_bias[None]
    )
    return (normed, split_heads, scores)


def attend_values(probs_low, split_heads):
    attended = jnp.einsum(
        "bhij,bjhc->bihc", probs_low, split_heads[2], preferred_element_type=jnp.float32
    )
    shape_now = attended.shape
    return attended.reshape(shape_now[0] * shape_now[1], shape_now[2] * shape_now[3]).astype(
        jnp.bfloat16
    )


def layer_forward(hidden, choose, params, position_bias, seq_len):
    gain_attn, w_qkv, w_out, gain_ffn, w_router, w_in, w_down = params
    normed, split_heads, scores = attend_scores(hidden, gain_attn, w_qkv, position_bias, seq_len)
    row_top = jnp.max(scores, axis=-1, keepdims=True)
    log_total = row_top + jnp.log(jnp.sum(jnp.exp(scores - row_top), axis=-1, keepdims=True))
    attended = attend_values(jnp.exp(scores - log_total).astype(jnp.bfloat16), split_heads)
    partial_attn = jnp.dot(attended, w_out, preferred_element_type=jnp.float32)
    middle = hidden + lax.psum(partial_attn.astype(jnp.bfloat16), "tensor").astype(jnp.float32)
    normed_ffn = rms_apply(middle, gain_ffn).astype(jnp.bfloat16)
    gate_value = route_gate(normed_ffn.astype(jnp.float32), w_router.astype(jnp.float32), choose)
    pre_act = jnp.einsum("rd,edf->erf", normed_ffn, w_in, preferred_element_type=jnp.float32)
    activated = jax.nn.gelu(pre_act).astype(jnp.bfloat16)
    expert_out = jnp.einsum("erf,efd->erd", activated, w_down, preferred_element_type=jnp.float32)
    partial_ffn = jnp.sum(expert_out * choose.T[:, :, None], axis=0)
    combined = lax.psum(partial_ffn.astype(jnp.bfloat16), "tensor").astype(jnp.float32)
    return (middle + gate_value * combined, (hidden, middle, log_total, combined, pre_act))


def ffn_backward(saved, choose, params, grad_top):
    gain_attn, w_qkv, w_out, gain_ffn, w_router, w_in, w_down = params
    hidden, middle, log_total, combined, kept_act = saved
    normed_ffn = rms_apply(middle, gain_ffn).astype(jnp.bfloat16)

    def gate_local(normed_wide, router_wide):
        return route_gate(normed_wide, router_wide, choose)

    gate_value, gate_pull = jax.vjp(
        gate_local, normed_ffn.astype(jnp.float32), w_router.astype(jnp.float32)
    )
    grad_gate = jnp.sum(grad_top * combined, axis=-1, keepdims=True)
    grad_comb = (gate_value * grad_top).astype(jnp.bfloat16)
    grad_expert = choose.T[:, :, None].astype(jnp.bfloat16) * grad_comb[None]
    activated, act_pull = jax.vjp(jax.nn.gelu, kept_act)
    grad_down = jnp.einsum(
        "erf,erd->efd",
        activated.astype(jnp.bfloat16),
        grad_expert,
        preferred_element_type=jnp.float32,
    )
    grad_activ = jnp.einsum("erd,efd->erf", grad_expert, w_down, preferred_element_type=jnp.float32)
    grad_pre = act_pull(grad_activ)[0].astype(jnp.bfloat16)
    grad_in = jnp.einsum("rd,erf->edf", normed_ffn, grad_pre, preferred_element_type=jnp.float32)
    partial_back = jnp.einsum("erf,edf->rd", grad_pre, w_in, preferred_element_type=jnp.float32)
    grad_normed = lax.psum(partial_back.astype(jnp.bfloat16), "tensor").astype(jnp.float32)
    grad_wide, grad_router = gate_pull(grad_gate)
    grad_normed = grad_normed + grad_wide
    unused_val, norm_pull = jax.vjp(rms_apply, middle, gain_ffn)
    grad_middle, grad_gain = norm_pull(grad_normed)
    return (grad_top + grad_middle, (grad_gain, grad_router, grad_in, grad_down))


def attn_backward(saved, params, position_bias, onehot_low, seq_len, grad_mid):
    gain_attn, w_qkv, w_out, gain_ffn, w_router, w_in, w_down = params
    hidden, middle, log_total, combined, kept_act = saved
    normed, split_heads, scores = attend_scores(hidden, gain_attn, w_qkv, position_bias, seq_len)
    probs = jnp.exp(scores - log_total)
    probs_low = probs.astype(jnp.bfloat16)
    attended = attend_values(probs_low, split_heads)
    grad_branch = grad_mid.astype(jnp.bfloat16)
    grad_wout = jnp.einsum("rc,rd->cd", attended, grad_branch, preferred_element_type=jnp.float32)
    grad_att = jnp.einsum("rd,cd->rc", grad_branch, w_out, preferred_element_type=jnp.float32)
    grad_att = grad_att.astype(jnp.bfloat16).reshape(split_heads[0].shape)
    grad_probs = jnp.einsum(
        "bihc,bjhc->bhij", grad_att, split_heads[2], preferred_element_type=jnp.float32
    )
    inner = jnp.sum(probs * grad_probs, axis=-1, keepdims=True)
    grad_scores = (probs * (grad_probs - inner)).astype(jnp.bfloat16)
    grad_table = jnp.einsum(
        "bhij,nij->nh", grad_scores, onehot_low, preferred_element_type=jnp.float32
    )
    grad_value = jnp.einsum(
        "bhij,bihc->bjhc", probs_low, grad_att, preferred_element_type=jnp.float32
    )
    grad_query = (
        jnp.einsum(
            "bhij,bjhc->bihc", grad_scores, split_heads[1], preferred_element_type=jnp.float32
        )
        * score_scale
    )
    grad_key = (
        jnp.einsum(
            "bhij,bihc->bjhc", grad_scores, split_heads[0], preferred_element_type=jnp.float32
        )
        * score_scale
    )
    row_count = hidden.shape[0]
    grad_proj = (
        jnp.stack([grad_query, grad_key, grad_value]).astype(jnp.bfloat16).reshape(3, row_count, -1)
    )
    grad_qkv = jnp.einsum("rd,krc->kdc", normed, grad_proj, preferred_element_type=jnp.float32)
    partial_back = jnp.einsum("krc,kdc->rd", grad_proj, w_qkv, preferred_element_type=jnp.float32)
    grad_normed = lax.psum(partial_back.astype(jnp.bfloat16), "tensor").astype(jnp.float32)
    unused_val, norm_pull = jax.vjp(rms_apply, hidden, gain_attn)
    grad_hidden, grad_gain = norm_pull(grad_normed)
    return (grad_mid + grad_hidden, (grad_table, grad_gain, grad_qkv, grad_wout))


def add_masked(running, extra, active):
    masked = tuple((jnp.where(active, member, jnp.zeros_like(member)) for member in extra))
    if running is None:
        return masked
    return tuple((summed + member for summed, member in zip(running, masked)))


def shards(
    embedded,
    expert_index,
    buckets,
    rel_bias,
    gain_attn,
    w_qkv,
    w_out,
    gain_ffn,
    w_router,
    w_in,
    w_down,
    cotangent,
):
    first_section = lax.axis_index("section") == 0
    params = (gain_attn[0], w_qkv[0], w_out[0], gain_ffn[0], w_router[0], w_in[0], w_down[0])
    seq_len = buckets.shape[0]
    bucket_count = rel_bias.shape[0]
    onehot_low = (buckets[None] == jnp.arange(bucket_count, dtype=jnp.int32)[:, None, None]).astype(
        jnp.bfloat16
    )
    position_bias = jnp.einsum(
        "nij,nh->hij", onehot_low.astype(jnp.float32), rel_bias, precision=exact_mode
    )
    batch_rows = embedded.shape[0] // MB
    model_width = embedded.shape[1]
    expert_count = w_router.shape[2]
    choose_all = (expert_index[0] == jnp.arange(expert_count, dtype=jnp.int32)[None, :]).astype(
        jnp.float32
    )

    def rows_of(source, batch_index):
        start = min(max(batch_index, 0), MB - 1) * batch_rows
        return source[start : start + batch_rows]

    received = jnp.zeros((batch_rows, model_width), jnp.bfloat16)
    outputs = []
    saved_all = []
    for tick_index in range(MB + 1):
        route_rows = jnp.where(
            first_section, rows_of(choose_all, tick_index), rows_of(choose_all, tick_index - 1)
        )
        layer_in = jnp.where(first_section, rows_of(embedded, tick_index), received).astype(
            jnp.float32
        )
        layer_out, saved = layer_forward(layer_in, route_rows, params, position_bias, seq_len)
        outputs.append(layer_out)
        saved_all.append((saved, route_rows))
        if tick_index < MB:
            received = from_behind(layer_out.astype(jnp.bfloat16), "section", 1)
    grad_recv = jnp.zeros((batch_rows, model_width), jnp.bfloat16)
    ffn_totals = None
    attn_totals = None
    grad_inputs = []
    for tick_index in range(MB + 1):
        saved, route_rows = saved_all[MB - tick_index]
        grad_top = jnp.where(
            first_section, grad_recv, rows_of(cotangent, MB - 1 - tick_index)
        ).astype(jnp.float32)
        active = jnp.where(first_section, tick_index >= 1, tick_index < MB)
        grad_mid, ffn_grads = ffn_backward(saved, route_rows, params, grad_top)
        ffn_totals = add_masked(ffn_totals, ffn_grads, active)
        grad_layer_in, attn_grads = attn_backward(
            saved, params, position_bias, onehot_low, seq_len, grad_mid
        )
        attn_totals = add_masked(attn_totals, attn_grads, active)
        grad_inputs.append(grad_layer_in)
        if tick_index < MB:
            grad_recv = from_behind(grad_layer_in.astype(jnp.bfloat16), "section", -1)
    table_sum, attn_gain_sum, qkv_sum, wout_sum, ffn_gain_sum, router_sum, win_sum, down_sum = (
        lax.psum(attn_totals[0].astype(jnp.bfloat16), "dp").astype(jnp.float32),
        lax.psum(attn_totals[1].astype(jnp.bfloat16), "dp").astype(jnp.float32),
        lax.psum(attn_totals[2].astype(jnp.bfloat16), "dp").astype(jnp.float32),
        lax.psum(attn_totals[3].astype(jnp.bfloat16), "dp").astype(jnp.float32),
        lax.psum(ffn_totals[0].astype(jnp.bfloat16), "dp").astype(jnp.float32),
        lax.psum(ffn_totals[1].astype(jnp.bfloat16), "dp").astype(jnp.float32),
        lax.psum(ffn_totals[2].astype(jnp.bfloat16), "dp").astype(jnp.float32),
        lax.psum(ffn_totals[3].astype(jnp.bfloat16), "dp").astype(jnp.float32),
    )
    table_sum = lax.psum(table_sum, "section")
    hidden_rows = jnp.concatenate(
        [
            jnp.where(first_section, outputs[batch_index], outputs[batch_index + 1])
            for batch_index in range(MB)
        ],
        axis=0,
    )
    grad_rows = jnp.concatenate(
        [
            jnp.where(
                first_section, grad_inputs[MB - batch_index], grad_inputs[MB - 1 - batch_index]
            )
            for batch_index in range(MB)
        ],
        axis=0,
    )
    return (
        hidden_rows[None],
        grad_rows[None],
        table_sum,
        attn_gain_sum[None],
        qkv_sum[None],
        wout_sum[None],
        ffn_gain_sum[None],
        router_sum[None],
        win_sum[None],
        down_sum[None],
    )


def solution(mesh):
    in_specs = (
        P("dp", None),
        P("section", "dp", None),
        P(),
        P(None, "tensor"),
        P("section", None),
        P("section", None, None, "tensor"),
        P("section", "tensor", None),
        P("section", None),
        P("section", None, None),
        P("section", None, None, "tensor"),
        P("section", None, "tensor", None),
        P("dp", None),
    )
    out_specs = (
        P("section", "dp", None),
        P("section", "dp", None),
        P(None, "tensor"),
        P("section", None),
        P("section", None, None, "tensor"),
        P("section", "tensor", None),
        P("section", None),
        P("section", None, None),
        P("section", None, None, "tensor"),
        P("section", None, "tensor", None),
    )
    return jax.shard_map(shards, mesh=mesh, in_specs=in_specs, out_specs=out_specs, check_vma=False)
```

profile of v0, /device:TPU:0, one launch (start us, length us, event | category | flops | bytes accessed | tf_op | source)
XLA Modules:
  0.0 899.9 jit_solution(5121509498083767465)
XLA Ops:
  22.0 43.7 %all-reduce.16.cloned.1.call-done = bf16[256,768]{1,0:T(8,128)(2,1)} async-done(((bf16[256,768]{1,0:T(8,128)(2,1)}), bf16[256,768]{1,0:T(8,128)(2,1)}) %all-reduce.16.cloned.1.call-update) | async-done | bytes 393232 | tf_op jit(solution)/shard_map/psum | solution.py:72
  73.7 42.9 %all-reduce.18.cloned.1.call-done = bf16[256,768]{1,0:T(8,128)(2,1)} async-done(((bf16[256,768]{1,0:T(8,128)(2,1)}), bf16[256,768]{1,0:T(8,128)(2,1)}) %all-reduce.18.cloned.1.call-update) | async-done | bytes 393232 | tf_op jit(solution)/shard_map/psum | solution.py:79
  117.9 4.9 collective-permute-start
  122.8 6.2 collective-permute-done
  140.3 44.2 %all-reduce.20.cloned.1.call-done = bf16[256,768]{1,0:T(8,128)(2,1)} async-done(((bf16[256,768]{1,0:T(8,128)(2,1)}), bf16[256,768]{1,0:T(8,128)(2,1)}) %all-reduce.20.cloned.1.call-update) | async-done | bytes 393232 | tf_op jit(solution)/shard_map/psum | solution.py:72
  188.1 2.6 fusion.22
  197.9 38.6 %all-reduce.22.cloned.1.call-done = bf16[256,768]{1,0:T(8,128)(2,1)} async-done(((bf16[256,768]{1,0:T(8,128)(2,1)}), bf16[256,768]{1,0:T(8,128)(2,1)}) %all-reduce.22.cloned.1.call-update) | async-done | bytes 393232 | tf_op jit(solution)/shard_map/psum | solution.py:79
  236.5 2.7 fusion.177
  239.2 4.9 collective-permute-start.1
  245.4 5.2 collective-permute-done.1
  258.8 2.0 convolution_convert_fusion
  263.5 41.4 %all-reduce.24.cloned.1.call-done = bf16[256,768]{1,0:T(8,128)(2,1)} async-done(((bf16[256,768]{1,0:T(8,128)(2,1)}), bf16[256,768]{1,0:T(8,128)(2,1)}) %all-reduce.24.cloned.1.call-update) | async-done | bytes 393232 | tf_op jit(solution)/shard_map/psum | solution.py:72
  308.5 2.6 fusion.20
  317.0 40.0 %all-reduce.26.cloned.1.call-done = bf16[256,768]{1,0:T(8,128)(2,1)} async-done(((bf16[256,768]{1,0:T(8,128)(2,1)}), bf16[256,768]{1,0:T(8,128)(2,1)}) %all-reduce.26.cloned.1.call-update) | async-done | bytes 393232 | tf_op jit(solution)/shard_map/psum | solution.py:79
  368.7 40.3 %all-reduce.28.cloned.1.call-done = bf16[256,768]{1,0:T(8,128)(2,1)} async-done(((bf16[256,768]{1,0:T(8,128)(2,1)}), bf16[256,768]{1,0:T(8,128)(2,1)}) %all-reduce.28.cloned.1.call-update) | async-done | bytes 393232 | tf_op jit(solution)/shard_map/psum | solution.py:108
  409.0 2.6 multiply_reduce_fusion.5
  427.9 2.4 fusion.83
  430.4 4.6 fusion.135
  435.0 38.3 %all-reduce.30.cloned.1.call-done = bf16[256,768]{1,0:T(8,128)(2,1)} async-done(((bf16[256,768]{1,0:T(8,128)(2,1)}), bf16[256,768]{1,0:T(8,128)(2,1)}) %all-reduce.30.cloned.1.call-update) | async-done | bytes 393232 | tf_op jit(solution)/shard_map/psum | solution.py:156
  473.3 2.0 fusion.158
  479.7 3.0 fusion.184
  484.6 5.7 collective-permute-done.2
  498.1 39.2 %all-reduce.32.cloned.1.call-done = bf16[256,768]{1,0:T(8,128)(2,1)} async-done(((bf16[256,768]{1,0:T(8,128)(2,1)}), bf16[256,768]{1,0:T(8,128)(2,1)}) %all-reduce.32.cloned.1.call-update) | async-done | bytes 393232 | tf_op jit(solution)/shard_map/psum | solution.py:108
  537.3 2.5 multiply_reduce_fusion.4
  551.2 2.5 fusion.84
  553.8 2.3 convolution_select_fusion.1
  556.1 3.0 fusion.187
  559.1 37.5 %all-reduce.34.cloned.1.call-done = bf16[256,768]{1,0:T(8,128)(2,1)} async-done(((bf16[256,768]{1,0:T(8,128)(2,1)}), bf16[256,768]{1,0:T(8,128)(2,1)}) %all-reduce.34.cloned.1.call-update) | async-done | bytes 393232 | tf_op jit(solution)/shard_map/psum | solution.py:156
  599.3 2.4 fusion.312
  603.5 3.2 fusion.132
  606.7 7.2 collective-permute-done.3
  619.2 5.8 fusion.1
  625.1 4.8 fusion
  630.0 30.9 %all-reduce.36.cloned.1.call-done = bf16[256,768]{1,0:T(8,128)(2,1)} async-done(((bf16[256,768]{1,0:T(8,128)(2,1)}), bf16[256,768]{1,0:T(8,128)(2,1)}) %all-reduce.36.cloned.1.call-update) | async-done | bytes 393232 | tf_op jit(solution)/shard_map/psum | solution.py:108
  660.9 2.7 multiply_reduce_fusion.3
  677.0 2.4 fusion.85
  679.4 2.7 fusion.179
  682.5 2.6 fusion.99
  685.1 3.0 fusion.66
  695.0 2.7 maximum_bitcast_fusion
  700.8 24.3 %all-reduce.38.cloned.1.call-done = bf16[256,768]{1,0:T(8,128)(2,1)} async-done(((bf16[256,768]{1,0:T(8,128)(2,1)}), bf16[256,768]{1,0:T(8,128)(2,1)}) %all-reduce.38.cloned.1.call-update) | async-done | bytes 393232 | tf_op jit(solution)/shard_map/psum | solution.py:156
  727.3 54.2 %all-reduce = (bf16[32,3]{0,1:T(4,128)(2,1)S(1)}, bf16[1,768]{1,0:T(2,128)(2,1)S(1)}, bf16[1,768]{1,0:T(2,128)(2,1)S(1)}, bf16[1,768,2]{1,2,0:T(2,128)(2,1)S(1)}) all-reduce(bf16[32,3]{0,1:T(4,128)(2,1)S(1)} %fusion.127, bf16[1,768]{1,0:T(2,128)(2,1)S(1)} %broadcast_in_dim.86, ...), channel_id=1, replica_groups=mesh['section'=2,'tensor'=4,'dp'=16] {'dp'}, use_global_device_ids=true, to_apply=%region_60.61 | all-reduce | flops 3168 | bytes 12672 | tf_op jit(solution)/shard_map/psum | solution.py:239
  783.2 7.0 psum.160
  790.3 2.4 fusion.170
  793.9 85.8 %all-reduce.40.cloned.1.call-done = (bf16[1,2,768,768]{2,3,1,0:T(8,128)(2,1)}, bf16[1,3,768,192]{2,3,1,0:T(8,128)(2,1)}, bf16[1,192,768]{2,1,0:T(8,128)(2,1)}, bf16[1,2,768,768]{3,2,1,0:T(8,128)(2,1)}) async-done(((bf16[1,2,768,768]{2,3,1,0:T(8,128)(2,1)}, bf16[1,3,768,192]{2,3,1,0:T(8,128)(2,1)}, bf16[1,192,768]{2,1,0:T(8,128)(2,1)}, bf16[1,2,768,768]{3,2,1,0:T(8,128)(2,1)}), ...) | async-done | bytes 5898256 | tf_op jit(solution)/shard_map/psum | solution.py:245
  881.5 2.5 broadcast_in_dim.89
  884.1 4.6 copy.180
  888.6 4.2 broadcast_in_dim.189
  (517 shorter events, 160.0 us)
Async XLA Ops:
  7.2 64.8 %copy-start = (bf16[1,2,768,768]{3,2,1,0:T(8,128)(2,1)S(1)}, bf16[1,2,768,768]{3,2,1,0:T(8,128)(2,1)}, u32[]{:S(2)}) copy-start(bf16[1,2,768,768]{3,2,1,0:T(8,128)(2,1)} %param.22) | copy-start | bytes 7077892
  7.2 58.5 %all-reduce.16.cloned.1.call-start = ((), (), s32[]{:S(2)}) async-start(), calls=%async_computation | async-start | bytes 786432 | tf_op jit(solution)/shard_map/psum | solution.py:72
  15.5 50.2 %copy-start.1 = (bf16[512,768]{1,0:T(8,128)(2,1)S(1)}, bf16[512,768]{1,0:T(8,128)(2,1)}, u32[]{:S(2)}) copy-start(bf16[512,768]{1,0:T(8,128)(2,1)} %param.12) | copy-start | bytes 2359300
  19.5 50.0 %copy-start.96 = (bf16[1,768,2]{1,2,0:T(2,128)(2,1)S(1)}, bf16[1,768,2]{1,2,0:T(2,128)(2,1)}, u32[]{:S(2)}) copy-start(bf16[1,768,2]{1,2,0:T(2,128)(2,1)} %param.20) | copy-start | bytes 9220
  20.5 96.1 %all-reduce.18.cloned.1.call-start = ((), (), s32[]{:S(2)}) async-start(), calls=%async_computation.1 | async-start | bytes 786432 | tf_op jit(solution)/shard_map/psum | solution.py:79
  22.0 48.6 %copy-start.83 = (f32[512,2]{0,1:T(2,128)}, f32[512,2]{0,1:T(2,128)S(1)}, u32[]{:S(2)}) copy-start(f32[512,2]{0,1:T(2,128)S(1)} %compare_convert_fusion) | copy-start | bytes 12292
  71.9 44.7 %copy-start.105 = (f32[256]{0:T(256)}, f32[256]{0:T(256)S(1)}, u32[]{:S(2)}) copy-start(f32[256]{0:T(256)S(1)} %get-tuple-element.118) | copy-start | bytes 3076
  71.9 44.7 %copy-start.29 = (bf16[256,768]{1,0:T(8,128)(2,1)S(1)}, bf16[256,768]{1,0:T(8,128)(2,1)}, u32[]{:S(2)}) copy-start(bf16[256,768]{1,0:T(8,128)(2,1)} %all-reduce.16.cloned.1.call-done) | copy-start | bytes 1179652
  73.7 110.8 %all-reduce.20.cloned.1.call-start = ((), (), s32[]{:S(2)}) async-start(), calls=%async_computation.2 | async-start | bytes 786432 | tf_op jit(solution)/shard_map/psum | solution.py:72
  116.6 12.7 %copy-start.44 = (bf16[1,3,768,192]{2,3,1,0:T(8,128)(2,1)S(1)}, bf16[1,3,768,192]{2,3,1,0:T(8,128)(2,1)}, u32[]{:S(2)}) copy-start(bf16[1,3,768,192]{2,3,1,0:T(8,128)(2,1)} %param.17) | copy-start | bytes 2654212
  117.9 11.1 %collective-permute-start = (bf16[256,768]{1,0:T(8,128)(2,1)S(1)}, bf16[256,768]{1,0:T(8,128)(2,1)S(1)}, u32[]{:S(2)}, u32[]{:S(2)}) collective-permute-start(bf16[256,768]{1,0:T(8,128)(2,1)S(1)} %fusion.178), channel_id=1, source_target_pairs={{0,64},{1,65},{2,66},{3,67},{4,68},{5,69},{6,70},{7,71},{8,72},{9,... | collective-permute-start | bytes 1179656 | tf_op jit(solution)/shard_map/ppermute | solution.py:17
  140.3 96.2 %all-reduce.22.cloned.1.call-start = ((), (), s32[]{:S(2)}) async-start(), calls=%async_computation.3 | async-start | bytes 786432 | tf_op jit(solution)/shard_map/psum | solution.py:79
  193.6 111.4 %all-reduce.24.cloned.1.call-start = ((), (), s32[]{:S(2)}) async-start(), calls=%async_computation.4 | async-start | bytes 786432 | tf_op jit(solution)/shard_map/psum | solution.py:72
  239.2 11.4 %collective-permute-start.1 = (bf16[256,768]{1,0:T(8,128)(2,1)}, bf16[256,768]{1,0:T(8,128)(2,1)S(1)}, u32[]{:S(2)}, u32[]{:S(2)}) collective-permute-start(bf16[256,768]{1,0:T(8,128)(2,1)} %get-tuple-element.93), channel_id=1, source_target_pairs={{0,64},{1,65},{2,66},{3,67},{4,68},{5,69},{6,70},{7,71},{8,72},{9,... | collective-permute-start | bytes 1179656 | tf_op jit(solution)/shard_map/ppermute | solution.py:17
  260.9 96.1 %all-reduce.26.cloned.1.call-start = ((), (), s32[]{:S(2)}) async-start(), calls=%async_computation.5 | async-start | bytes 786432 | tf_op jit(solution)/shard_map/psum | solution.py:79
  313.9 95.0 %all-reduce.28.cloned.1.call-start = ((), (), s32[]{:S(2)}) async-start(), calls=%async_computation.6 | async-start | bytes 786432 | tf_op jit(solution)/shard_map/psum | solution.py:108
  366.0 107.2 %all-reduce.30.cloned.1.call-start = ((), (), s32[]{:S(2)}) async-start(), calls=%async_computation.7 | async-start | bytes 786432 | tf_op jit(solution)/shard_map/psum | solution.py:156
  421.2 9.2 %copy-start.62 = (bf16[256,768]{1,0:T(8,128)(2,1)S(1)}, bf16[256,768]{1,0:T(8,128)(2,1)}, u32[]{:S(2)}) copy-start(bf16[256,768]{1,0:T(8,128)(2,1)} %copy-done.61) | copy-start | bytes 1179652
  430.3 106.9 %all-reduce.32.cloned.1.call-start = ((), (), s32[]{:S(2)}) async-start(), calls=%async_computation.8 | async-start | bytes 786432 | tf_op jit(solution)/shard_map/psum | solution.py:108
  435.0 44.7 %copy-start.27 = (bf16[256,768]{1,0:T(8,128)(2,1)S(1)}, bf16[256,768]{1,0:T(8,128)(2,1)}, u32[]{:S(2)}) copy-start(bf16[256,768]{1,0:T(8,128)(2,1)} %copy-done.26) | copy-start | bytes 1179652
  478.1 12.2 %collective-permute-start.2 = (bf16[256,768]{1,0:T(8,128)(2,1)S(1)}, bf16[256,768]{1,0:T(8,128)(2,1)S(1)}, u32[]{:S(2)}, u32[]{:S(2)}) collective-permute-start(bf16[256,768]{1,0:T(8,128)(2,1)S(1)} %fusion.304), channel_id=1, source_target_pairs={{64,0},{65,1},{66,2},{67,3},{68,4},{69,5},{70,6},{71,7},{72,8},{73... | collective-permute-start | bytes 1179656 | tf_op jit(solution)/shard_map/ppermute | solution.py:17
  482.8 7.8 copy-start.89
  482.8 8.5 copy-start.116
  493.9 43.4 %copy-start.38 = (bf16[256,768]{1,0:T(8,128)(2,1)S(1)}, bf16[256,768]{1,0:T(8,128)(2,1)}, u32[]{:S(2)}) copy-start(bf16[256,768]{1,0:T(8,128)(2,1)} %all-reduce.20.cloned.1.call-done) | copy-start | bytes 1179652
  495.5 101.1 %all-reduce.34.cloned.1.call-start = ((), (), s32[]{:S(2)}) async-start(), calls=%async_computation.9 | async-start | bytes 786432 | tf_op jit(solution)/shard_map/psum | solution.py:156
  553.7 107.2 %all-reduce.36.cloned.1.call-start = ((), (), s32[]{:S(2)}) async-start(), calls=%async_computation.10 | async-start | bytes 786432 | tf_op jit(solution)/shard_map/psum | solution.py:108
  556.1 40.5 %copy-start.103 = (f32[256]{0:T(256)S(1)}, f32[256]{0:T(256)}, u32[]{:S(2)}) copy-start(f32[256]{0:T(256)} %copy-done.102) | copy-start | bytes 3076
  601.7 12.2 %copy-start.43 = (bf16[512,768]{1,0:T(8,128)(2,1)S(1)}, bf16[512,768]{1,0:T(8,128)(2,1)}, u32[]{:S(2)}) copy-start(bf16[512,768]{1,0:T(8,128)(2,1)} %param.23) | copy-start | bytes 2359300
  601.7 12.2 %copy-start.45 = (bf16[256,768]{1,0:T(8,128)(2,1)S(1)}, bf16[256,768]{1,0:T(8,128)(2,1)}, u32[]{:S(2)}) copy-start(bf16[256,768]{1,0:T(8,128)(2,1)} %all-reduce.18.cloned.1.call-done) | copy-start | bytes 1179652
  601.7 12.2 %collective-permute-start.3 = (bf16[256,768]{1,0:T(8,128)(2,1)S(1)}, bf16[256,768]{1,0:T(8,128)(2,1)S(1)}, u32[]{:S(2)}, u32[]{:S(2)}) collective-permute-start(bf16[256,768]{1,0:T(8,128)(2,1)S(1)} %get-tuple-element.74), channel_id=1, source_target_pairs={{64,0},{65,1},{66,2},{67,3},{68,4},{69,5},{70,6},{71,7},{72,8},{73... | collective-permute-start | bytes 1179656 | tf_op jit(solution)/shard_map/ppermute | solution.py:17
  603.4 10.8 %copy-start.84 = (f32[512,2]{0,1:T(2,128)S(1)}, f32[512,2]{0,1:T(2,128)}, u32[]{:S(2)}) copy-start(f32[512,2]{0,1:T(2,128)} %copy-done.83) | copy-start | bytes 12292
  603.4 10.8 %copy-start.149 = (f32[256]{0:T(256)S(1)}, f32[256]{0:T(256)}, u32[]{:S(2)}) copy-start(f32[256]{0:T(256)} %multiply_divide_fusion) | copy-start | bytes 3076
  606.7 8.2 copy-start.106
  606.7 8.4 copy-start.37
  606.7 8.4 copy-start.147
  619.1 105.9 %all-reduce.38.cloned.1.call-start = ((), (), s32[]{:S(2)}) async-start(), calls=%async_computation.11 | async-start | bytes 786432 | tf_op jit(solution)/shard_map/psum | solution.py:156
  629.9 33.7 %copy-start.123 = (f32[256]{0:T(256)S(1)}, f32[256]{0:T(256)}, u32[]{:S(2)}) copy-start(f32[256]{0:T(256)} %copy-done.122) | copy-start | bytes 3076
  629.9 33.7 %copy-start.142 = (f32[256,2]{0,1:T(2,128)}, f32[256,2]{0,1:T(2,128)S(1)}, u32[]{:S(2)}) copy-start(f32[256,2]{0,1:T(2,128)S(1)} %get-tuple-element.69) | copy-start | bytes 6148
  629.9 33.7 %copy-start.119 = (f32[256]{0:T(256)S(1)}, f32[256]{0:T(256)}, u32[]{:S(2)}) copy-start(f32[256]{0:T(256)} %copy-done.118) | copy-start | bytes 3076
  630.0 33.7 %copy-start.145 = (f32[256]{0:T(256)}, f32[256]{0:T(256)S(1)}, u32[]{:S(2)}) copy-start(f32[256]{0:T(256)S(1)} %negate_divide_fusion) | copy-start | bytes 3076
  682.1 197.6 %all-reduce.40.cloned.1.call-start = ((), (), s32[]{:S(2)}) async-start(), calls=%async_computation.12 | async-start | bytes 11796480 | tf_op jit(solution)/shard_map/psum | solution.py:245
  697.7 28.8 %copy-start.107 = (f32[768]{0:T(1024)S(1)}, f32[768]{0:T(1024)}, u32[]{:S(2)}) copy-start(f32[768]{0:T(1024)} %get-tuple-element.48) | copy-start | bytes 9220
  697.7 28.8 %copy-start.108 = (f32[768]{0:T(1024)S(1)}, f32[768]{0:T(1024)}, u32[]{:S(2)}) copy-start(f32[768]{0:T(1024)} %get-tuple-element.50) | copy-start | bytes 9220
  697.7 92.5 %copy-start.121 = (f32[256]{0:T(256)S(1)}, f32[256]{0:T(256)}, u32[]{:S(2)}) copy-start(f32[256]{0:T(256)} %copy-done.120) | copy-start | bytes 3076
  697.7 92.5 %copy-start.46 = (bf16[256,768]{1,0:T(8,128)(2,1)S(1)}, bf16[256,768]{1,0:T(8,128)(2,1)}, u32[]{:S(2)}) copy-start(bf16[256,768]{1,0:T(8,128)(2,1)} %all-reduce.30.cloned.1.call-done) | copy-start | bytes 1179652
  697.7 92.5 %copy-start.92 = (f32[256]{0:T(256)S(1)}, f32[256]{0:T(256)}, u32[]{:S(2)}) copy-start(f32[256]{0:T(256)} %copy-done.90) | copy-start | bytes 3076
  697.8 92.5 %copy-start.137 = (f32[256]{0:T(256)S(1)}, f32[256]{0:T(256)}, u32[]{:S(2)}) copy-start(f32[256]{0:T(256)} %copy-done.136) | copy-start | bytes 3076
  698.0 28.5 %copy-start.152 = (f32[768]{0:T(1024)S(1)}, f32[768]{0:T(1024)}, u32[]{:S(2)}) copy-start(f32[768]{0:T(1024)} %get-tuple-element.42) | copy-start | bytes 9220
  (126 other events, 361.0 us)
Sparse Core Ops, SparseCore 0:
  20.7 45.0 all-reduce.15
  73.8 42.7 all-reduce.17
  140.4 44.0 all-reduce.19
  193.7 42.7 all-reduce.21
  261.0 43.9 all-reduce.23
  314.1 42.8 all-reduce.25
  366.2 42.7 all-reduce.27
  430.5 42.7 all-reduce.29
  495.6 41.5 all-reduce.31
  553.8 42.7 all-reduce.33
  619.2 41.5 all-reduce.35
  682.2 42.7 all-reduce.37
  728.4 151.2 all-reduce.39
where the time goes:
time: 910 us; the launch traced here: 900 us
  waiting for transfers between devices  572 us (63%)
  matrix products  112 us (12%)
  other arithmetic  68.3 us (8%)
  blocking collectives  61.2 us (7%)
  local copies, waits for them, and re-layouts  55.8 us (6%)
  between operations  16.4 us (2%)
  starting transfers between devices  14.1 us (2%)
    psum x3, waiting for transfers between devices, layer_forward(): lax.psum(partial_attn.astype(jnp.bfloat16), 'tensor').astype(jnp.float32)  129 us
    psum x3, waiting for transfers between devices, layer_forward(): lax.psum(partial_ffn.astype(jnp.bfloat16), 'tensor').astype(jnp.float32)  121 us
    psum x3, waiting for transfers between devices, ffn_backward(): lax.psum(partial_back.astype(jnp.bfloat16), 'tensor').astype(jnp.float32)  110 us
    psum x3, waiting for transfers between devices, attn_backward(): lax.psum(partial_back.astype(jnp.bfloat16), 'tensor').astype(jnp.float32)  100 us
    psum x1, waiting for transfers between devices, shards(): lax.psum(ffn_totals[2].astype(jnp.bfloat16), 'dp').astype(jnp.float32)  85.8 us
    psum x1, blocking collectives, shards(): lax.psum(attn_totals[0].astype(jnp.bfloat16), 'dp').astype(jnp.float32)  54.2 us
    unnamed x321, local copies, waits for them, and re-layouts  28.7 us
    ppermute x4, waiting for transfers between devices, from_behind(): return lax.ppermute(x, axis, pairs)  24.4 us
  transfers between devices with their start and end apart: 17, of which 17 were waited for; matrix products, arithmetic and copies ran while one was open for 8% of the time, Pallas kernels for 0%

commit v1 on v0

v1 whole, which is shorter than its diff:
```python
import functools

import jax
import jax.numpy as jnp
from jax import lax
from jax.experimental import pallas as pl
from jax.experimental.pallas import tpu as pltpu
from jax.sharding import PartitionSpec as P

BF = jnp.bfloat16
F32 = jnp.float32
EPS = 1e-06
ROOT = 0.7978845608028654
CUBE = 0.044715
PLACE = {2: 0, 1: 1, 3: 2, 0: 3}
COPIES = 160


def dot(a, b):
    return jnp.dot(a, b, preferred_element_type=F32)


def dot_nt(a, b):
    return lax.dot_general(a, b, (((1,), (1,)), ((), ())), preferred_element_type=F32)


def dot_tn(a, b):
    return lax.dot_general(a, b, (((0,), (0,)), ((), ())), preferred_element_type=F32)


def wide(v):
    return v.astype(F32)


def inverse_rms(values):
    return lax.rsqrt(jnp.mean(values * values, axis=-1, keepdims=True) + EPS)


class Links:
    def __init__(self, send_sems, recv_sems):
        self.send_sems, self.recv_sems = send_sems, recv_sems
        self.used = 0
        self.pending = []

    def copy(self, src, dst, device, landing=None):
        slot = self.used
        self.used += 1
        make = functools.partial(
            pltpu.make_async_remote_copy,
            src_ref=src,
            send_sem=self.send_sems.at[slot],
            recv_sem=self.recv_sems.at[slot],
            device_id=device,
            device_id_type=pl.DeviceIdType.MESH,
        )
        out = make(dst_ref=dst)
        arriving = out if landing is None else make(dst_ref=landing)
        return out, arriving

    def send(self, src, dst, device, landing=None):
        out, arriving = self.copy(src, dst, device, landing)
        out.start()
        self.pending.append(out)
        return arriving

    def drain(self):
        for out in self.pending:
            out.wait_send()
        self.pending = []


class Gather:
    def __init__(self, links, local, remote, right, left):
        self.links, self.local, self.remote = links, local, remote
        self.right, self.left = right, left

    def start(self):
        send, local, remote = self.links.send, self.local, self.remote
        self.a_right = send(local(0, 0), remote(0, 0, 1), self.right, local(3, 0))
        self.b_left = send(local(0, 1), remote(0, 1, -1), self.left, local(1, 1))
        self.b_right = send(local(0, 1), remote(0, 1, 1), self.right, local(3, 1))
        self.a_left = send(local(0, 0), remote(0, 0, -1), self.left, local(1, 0))

    def forward(self):
        send, local, remote = self.links.send, self.local, self.remote
        self.a_right.wait_recv()
        self.a_far = send(local(3, 0), remote(3, 0, 1), self.right, local(2, 0))
        self.b_left.wait_recv()
        self.b_far = send(local(1, 1), remote(1, 1, -1), self.left, local(2, 1))

    def finish_near(self):
        self.b_right.wait_recv()
        self.a_left.wait_recv()

    def finish_far(self):
        self.a_far.wait_recv()
        self.b_far.wait_recv()

    def finish(self):
        self.finish_near()
        self.finish_far()


class Scatter:
    def __init__(self, links, part, landed, summed, right, left):
        self.links, self.part, self.landed, self.summed = links, part, landed, summed
        self.right, self.left = right, left

    def start_far(self):
        send, part, landed = self.links.send, self.part, self.landed
        self.far_a = send(part(2, 0), landed.at[0], self.right)
        self.far_b = send(part(2, 1), landed.at[1], self.left)

    def start_right(self):
        self.near_b = self.links.send(self.part(1, 1), self.landed.at[2], self.right)

    def start_left(self):
        self.near_a = self.links.send(self.part(3, 0), self.landed.at[3], self.left)

    def relay(self):
        send, part, landed, summed = self.links.send, self.part, self.landed, self.summed
        self.far_a.wait_recv()
        summed[0] = (wide(landed[0]) + wide(part(1, 0)[...])).astype(BF)
        self.sum_a = send(summed.at[0], landed.at[4], self.right)
        self.far_b.wait_recv()
        summed[1] = (wide(landed[1]) + wide(part(3, 1)[...])).astype(BF)
        self.sum_b = send(summed.at[1], landed.at[5], self.left)

    def finish(self):
        for arriving in (self.near_b, self.near_a, self.sum_a, self.sum_b):
            arriving.wait_recv()
        landed, part = self.landed, self.part
        top = wide(part(0, 0)[...]) + wide(landed[3]) + wide(landed[4])
        bottom = wide(part(0, 1)[...]) + wide(landed[2]) + wide(landed[5])
        return top, bottom


def kernel(
    embedded,
    expert_index,
    buckets,
    rel_bias,
    gain_attn,
    w_qkv,
    w_out,
    gain_ffn,
    router,
    w_in,
    w_down,
    cotangent,
    out_hidden,
    out_input,
    out_ffn,
    out_attn,
    out_small,
    x_all,
    n_attn,
    heads,
    probs,
    bias,
    att_all,
    w_out_all,
    middle,
    n_ffn,
    gate,
    expert,
    act,
    slope,
    part_a,
    part_b,
    part_c,
    landed_z,
    summed_z,
    combined,
    hidden_low,
    grad_top,
    grad_comb,
    grad_pre,
    grad_branch,
    grad_mid,
    input_low,
    grad_heads,
    grad_proj,
    table_rows,
    ffn_grads,
    attn_grads,
    ffn_pair,
    attn_pair,
    ffn_landed,
    attn_landed,
    ffn_summed,
    attn_summed,
    ffn_cross,
    attn_cross,
    small,
    small_z,
    small_y,
    small_xc,
    small_s,
    send_sems,
    recv_sems,
):
    section, t, d = lax.axis_index("section"), lax.axis_index("tensor"), lax.axis_index("dp")
    y, xl, c = d // 4, (d // 2) % 2, d % 2
    ztx = lambda k: {"tensor": (t + k) % 4}
    ydx = lambda k: {"dp": (d + 4 * k) % 16}
    x_mate, c_mate = {"dp": d + 2 - 4 * xl}, {"dp": d + 1 - 2 * c}
    xc_mate = {"dp": d + 2 - 4 * xl + 1 - 2 * c}
    s_mate = {"section": 1 - section}
    links = Links(send_sems, recv_sems)
    first, second = section == 0, section == 1

    barrier = pltpu.get_barrier_semaphore()
    mates = [ztx(1), ztx(2), ztx(3), ydx(1), ydx(2), ydx(3), x_mate, c_mate, xc_mate, s_mate]
    for mate in mates:
        pl.semaphore_signal(barrier, inc=1, device_id=mate, device_id_type=pl.DeviceIdType.MESH)

    def block(ref, k, rows=128):
        return ref.at[pl.ds(PLACE[k] * rows, rows)]

    def halves(ref):
        return lambda k, half: ref.at[pl.ds(PLACE[k] * 128 + half * 64, 64)]

    def halves_far(ref):
        return lambda k, half, way: ref.at[pl.ds(PLACE[(k - way) % 4] * 128 + half * 64, 64)]

    def own_order(ref):
        return lambda k, half: ref.at[pl.ds(((t + k) % 4) * 128 + half * 64, 64)]

    def own_order_far(ref):
        return lambda k, half, way: own_order(ref)(k, half)

    def z_gather(local, remote):
        return Gather(links, local, remote, ztx(1), ztx(3))

    for k in range(4):
        rows = pl.ds(PLACE[k] * 128, 128)
        theirs = pl.ds(((t + k) % 4) * 128, 128)
        expert[rows, :] = (expert_index[theirs, :] == 0).astype(F32)

        @pl.when(first)
        def _():
            x_all[rows, :] = embedded[theirs, :]

        @pl.when(second)
        def _():
            grad_top[rows, :] = cotangent[theirs, :]

    w_out_all[0] = w_out[...]
    which = buckets[...]
    for h in range(3):
        bias[h] = jnp.zeros((128, 128), F32)

    def add_bias(b, carry):
        hit = which == b
        for h in range(3):
            bias[h] = jnp.where(hit, rel_bias[b, h], bias[h])
        return carry

    lax.fori_loop(0, 32, add_bias, 0)
    pl.semaphore_wait(barrier, len(mates))

    w_gather = z_gather(
        lambda k, half: w_out_all.at[k, pl.ds(half * 96, 96)],
        lambda k, half, way: w_out_all.at[(k - way) % 4, pl.ds(half * 96, 96)],
    )
    w_gather.start()

    hop_out, hop_in = links.copy(hidden_low, x_all.at[pl.ds(PLACE[0] * 128, 128)], s_mate)

    @pl.when(first)
    def _():
        w_gather_done = None

    w_gather.forward()

    x_gather = z_gather(halves(x_all), halves_far(x_all))
    x_links = Links(send_sems, recv_sems)
    x_links.used = links.used
    links.used += 6
    x_gather.links = x_links

    @pl.when(second)
    def _():
        hop_in.wait_recv()
        x_gather.start()
        x_gather.forward()
        x_gather.finish()
        x_links.drain()

    for pair in (1, 0):
        rows = pl.ds(pair * 256, 256)
        values = wide(x_all[rows, :])
        normed = (values * inverse_rms(values) * gain_attn[...]).astype(BF)
        n_attn[rows, :] = normed
        for k in range(3):
            projected = dot(normed, w_qkv[k]).astype(BF)
            for h in range(3):
                heads[3 * k + h, rows, :] = projected[:, h * 64 : (h + 1) * 64]

    att_near_right, att_near_left = {}, {}
    for k in (0, 2, 1, 3):
        rows = pl.ds(PLACE[k] * 128, 128)
        for h in range(3):
            scores = dot_nt(heads[h, rows, :], heads[3 + h, rows, :]) * 0.125 + bias[h]
            powers = jnp.exp(scores - jnp.max(scores, axis=-1, keepdims=True))
            weights = powers / jnp.sum(powers, axis=-1, keepdims=True)
            probs[3 * k + h] = weights
            att_all[0, k, :, h * 64 : (h + 1) * 64] = dot(
                weights.astype(BF), heads[6 + h, rows, :]
            ).astype(BF)
        att_near_right[k] = links.send(
            att_all.at[0, k], att_all.at[3, (k - 1) % 4], ztx(1), att_all.at[3, k]
        )
        att_near_left[k] = links.send(
            att_all.at[0, k], att_all.at[1, (k + 1) % 4], ztx(3), att_all.at[1, k]
        )
    att_far = []
    for k in (0, 2, 1, 3):
        if k in (0, 1):
            m = (k - 1) % 4
            att_near_right[k].wait_recv()
            att_far.append(
                links.send(
                    att_all.at[3, m],
                    att_all.at[2, (m - 1) % 4],
                    ztx(1),
                    att_all.at[2, (m - 1) % 4],
                )
            )
        else:
            m = (k + 1) % 4
            att_near_left[k].wait_recv()
            att_far.append(
                links.send(
                    att_all.at[1, m],
                    att_all.at[2, (m + 1) % 4],
                    ztx(3),
                    att_all.at[2, (m + 1) % 4],
                )
            )
    for k in (2, 3):
        att_near_right[k].wait_recv()
    for k in (0, 1):
        att_near_left[k].wait_recv()
    w_gather.finish()
    for arriving in att_far:
        arriving.wait_recv()

    ffn_scatter = Scatter(
        links, halves(part_a), landed_z.at[0], summed_z.at[0], ztx(1), ztx(3)
    )
    for pair, ks in ((0, (2, 1)), (1, (3, 0))):
        rows = pl.ds(pair * 256, 256)
        total = wide(x_all[rows, :])
        for source in range(4):
            joined = jnp.concatenate([att_all[source, ks[0]], att_all[source, ks[1]]], axis=0)
            total = total + dot(joined, w_out_all[source])
        middle[rows, :] = total
        normed = (total * inverse_rms(total) * gain_ffn[...]).astype(BF)
        n_ffn[rows, :] = normed
        normed_wide = wide(normed)
        chosen = expert[rows, :]
        logit_gap = jnp.sum(normed_wide * router[0:1, :], axis=-1, keepdims=True) - jnp.sum(
            normed_wide * router[1:2, :], axis=-1, keepdims=True
        )
        gate[rows, :] = 1.0 / (1.0 + jnp.exp(jnp.where(chosen > 0.5, -logit_gap, logit_gap)))
        pre = jnp.where(chosen > 0.5, dot(normed, w_in[0]), dot(normed, w_in[1]))
        bent = jnp.tanh(ROOT * (pre + CUBE * pre * pre * pre))
        active = 0.5 * pre * (1.0 + bent)
        slope[rows, :] = 0.5 * (1.0 + bent) + 0.5 * pre * (1.0 - bent * bent) * ROOT * (
            1.0 + 3.0 * CUBE * pre * pre
        )
        active_low = active.astype(BF)
        act[rows, :] = active_low
        down = jnp.where(chosen > 0.5, dot(active_low, w_down[0]), dot(active_low, w_down[1]))
        part_a[rows, :] = down.astype(BF)
        if pair == 0:
            ffn_scatter.start_far()
            ffn_scatter.start_right()
        else:
            ffn_scatter.start_left()

    own = pl.ds(PLACE[0] * 128, 128)
    hidden_gather = z_gather(own_order(out_hidden), own_order_far(out_hidden))

    def end_forward():
        ffn_scatter.relay()
        top, bottom = ffn_scatter.finish()
        combined[0:64, :] = top
        combined[64:128, :] = bottom
        hidden_low[...] = (middle[own, :] + gate[own, :] * combined[...]).astype(BF)

    end_forward()

    @pl.when(first)
    def _():
        hop_out.start()

    out_hidden[pl.ds(t * 128, 128), :] = hidden_low[...]
    hidden_gather.start()
    hidden_gather.forward()

    back_out, back_in = links.copy(input_low, grad_top.at[pl.ds(PLACE[0] * 128, 128)], s_mate)
    top_gather = z_gather(halves(grad_top), halves_far(grad_top))
    top_links = Links(send_sems, recv_sems)
    top_links.used = links.used
    links.used += 6
    top_gather.links = top_links

    @pl.when(first)
    def _():
        hop_out.wait_send()
        back_in.wait_recv()
        top_gather.start()
        top_gather.forward()
        top_gather.finish()
        top_links.drain()

    back_scatter = Scatter(
        links, halves(part_b), landed_z.at[1], summed_z.at[1], ztx(1), ztx(3)
    )
    for pair in range(2):
        rows = pl.ds(pair * 256, 256)
        chosen = expert[rows, :]
        low = (gate[rows, :] * wide(grad_top[rows, :])).astype(BF)
        grad_comb[rows, :] = low
        into = jnp.where(chosen > 0.5, dot_nt(low, w_down[0]), dot_nt(low, w_down[1]))
        pre_low = (into * slope[rows, :]).astype(BF)
        grad_pre[rows, :] = pre_low
        back = jnp.where(chosen > 0.5, dot_nt(pre_low, w_in[0]), dot_nt(pre_low, w_in[1]))
        part_b[rows, :] = back.astype(BF)
        if pair == 0:
            back_scatter.start_far()
            back_scatter.start_right()
        else:
            back_scatter.start_left()
    back_scatter.relay()

    chosen_low = expert[...].astype(BF)
    other_low = (1.0 - expert[...]).astype(BF)
    for e, mask in enumerate((chosen_low, other_low)):
        ffn_grads[pl.ds(e * 768, 768), :] = dot_tn(n_ffn[...], grad_pre[...] * mask).astype(BF)
        ffn_grads[pl.ds(1536 + e * 768, 768), :] = dot_tn(act[...], grad_comb[...] * mask).astype(
            BF
        )

    class Reduce:
        def __init__(self, grads, pair_buf, landed, summed, cross, result):
            self.grads, self.pair_buf, self.cross, self.result = grads, pair_buf, cross, result
            rows = grads.shape[0]
            self.half, self.eighth, self.sixteenth = rows // 2, rows // 8, rows // 16
            self.scatter = Scatter(links, self.at(grads), landed, summed, ydx(1), ydx(3))
            local = self.at(result)
            self.gather = Gather(
                links, local, lambda k, half, way: local(k, half), ydx(1), ydx(3)
            )

        def at(self, ref):
            return lambda k, half: ref.at[
                pl.ds(
                    c * self.half + ((y + k) % 4) * self.eighth + half * self.sixteenth,
                    self.sixteenth,
                )
            ]

        def pair_start(self):
            theirs = self.grads.at[pl.ds((1 - c) * self.half, self.half)]
            self.paired = links.send(theirs, self.pair_buf, c_mate)

        def pair_finish(self):
            self.paired.wait_recv()
            step = 96

            def add(i, carry):
                mine = pl.ds(c * self.half + i * step, step)
                self.grads[mine, :] = (
                    wide(self.grads[mine, :]) + wide(self.pair_buf[pl.ds(i * step, step), :])
                ).astype(BF)
                return carry

            lax.fori_loop(0, self.half // step, add, 0)
            self.scatter.start_far()
            self.scatter.start_right()
            self.scatter.start_left()

        def relay(self):
            self.scatter.relay()

        def cross_start(self):
            top, bottom = self.scatter.finish()
            self.cross[0, 0 : self.sixteenth, :] = top.astype(BF)
            self.cross[0, self.sixteenth : self.eighth, :] = bottom.astype(BF)
            self.crossed = links.send(self.cross.at[0], self.cross.at[1], x_mate)

        def cross_finish(self):
            self.crossed.wait_recv()
            here = pl.ds(c * self.half + y * self.eighth, self.eighth)
            self.result[here, :] = (wide(self.cross[0]) + wide(self.cross[1])).astype(BF)
            self.gather.start()

        def forward(self):
            self.gather.forward()

        def share(self):
            self.gather.finish()
            mine = self.result.at[pl.ds(c * self.half, self.half)]
            theirs = self.result.at[pl.ds((1 - c) * self.half, self.half)]
            self.shared = links.send(mine, mine, c_mate, theirs)

        def finish(self):
            self.shared.wait_recv()

    ffn_sum = Reduce(ffn_grads, ffn_pair, ffn_landed, ffn_summed, ffn_cross, out_ffn)
    attn_sum = Reduce(attn_grads, attn_pair, attn_landed, attn_summed, attn_cross, out_attn)
    ffn_sum.pair_start()

    top, bottom = back_scatter.finish()
    from_units = jnp.concatenate([top, bottom], axis=0)
    top_own = wide(grad_top[own, :])
    grad_gate = jnp.sum(top_own * combined[...], axis=-1, keepdims=True)
    normed_own = wide(n_ffn[own, :])
    is_zero, gate_own = expert[own, :], gate[own, :]
    prob_zero = jnp.where(is_zero > 0.5, gate_own, 1.0 - gate_own)
    logit_zero = prob_zero * (is_zero - gate_own) * grad_gate
    logit_one = (1.0 - prob_zero) * (1.0 - is_zero - gate_own) * grad_gate
    small[...] = jnp.zeros_like(small)
    small[2:3, 0:768] = jnp.sum(normed_own * logit_zero, axis=0, keepdims=True)
    small[3:4, 0:768] = jnp.sum(normed_own * logit_one, axis=0, keepdims=True)
    grad_nffn = from_units + logit_zero * router[0:1, :] + logit_one * router[1:2, :]
    middle_own = middle[own, :]
    scale = inverse_rms(middle_own)
    small[1:2, 0:768] = jnp.sum(grad_nffn * middle_own * scale, axis=0, keepdims=True)
    g = grad_nffn * gain_ffn[...]
    inner = jnp.mean(g * middle_own, axis=-1, keepdims=True)
    grad_middle = top_own + scale * (g - middle_own * scale * scale * inner)
    grad_mid[...] = grad_middle
    grad_branch[own, :] = grad_middle.astype(BF)
    branch_gather = z_gather(halves(grad_branch), halves_far(grad_branch))
    branch_gather.start()
    ffn_sum.pair_finish()
    branch_gather.forward()
    branch_gather.finish()

    for pair in range(2):
        rows = pl.ds(pair * 256, 256)
        grad_att = dot_nt(grad_branch[rows, :], w_out[...]).astype(BF)
        for h in range(3):
            grad_heads[h, rows, :] = grad_att[:, h * 64 : (h + 1) * 64]
    table_rows[...] = jnp.zeros_like(table_rows)
    bias[...] = jnp.zeros_like(bias)
    attn_scatter = Scatter(
        links, halves(part_c), landed_z.at[2], summed_z.at[2], ztx(1), ztx(3)
    )
    for pair, ks in ((0, (2, 1)), (1, (3, 0))):
        for k in ks:
            rows = pl.ds(PLACE[k] * 128, 128)
            for h in range(3):
                weights = probs[3 * k + h]
                grad_att = grad_heads[h, rows, :]
                grad_w = dot_nt(grad_att, heads[6 + h, rows, :])
                mean = jnp.sum(weights * grad_w, axis=-1, keepdims=True)
                low = (weights * (grad_w - mean)).astype(BF)
                bias[h] += wide(low)
                at = h * 64
                grad_proj[rows, at : at + 64] = (0.125 * dot(low, heads[3 + h, rows, :])).astype(BF)
                at = 192 + h * 64
                grad_proj[rows, at : at + 64] = (0.125 * dot_tn(low, heads[h, rows, :])).astype(BF)
                at = 384 + h * 64
                grad_proj[rows, at : at + 64] = dot_tn(weights.astype(BF), grad_att).astype(BF)
        rows = pl.ds(pair * 256, 256)
        back = dot_nt(grad_proj[rows, 0:192], w_qkv[0])
        for k in range(1, 3):
            back = back + dot_nt(grad_proj[rows, k * 192 : (k + 1) * 192], w_qkv[k])
        part_c[rows, :] = back.astype(BF)
        if pair == 0:
            attn_scatter.start_far()
            attn_scatter.start_right()
        else:
            attn_scatter.start_left()
    attn_scatter.relay()
    ffn_sum.relay()

    attn_grads[0:576, :] = dot_tn(grad_proj[...], n_attn[...]).astype(BF)
    att_own = jnp.concatenate([att_all[0, k] for k in (2, 1, 3, 0)], axis=0)
    attn_grads[576:768, :] = dot_tn(att_own, grad_branch[...]).astype(BF)
    attn_sum.pair_start()

    top, bottom = attn_scatter.finish()
    grad_nattn = jnp.concatenate([top, bottom], axis=0)
    x_own = wide(x_all[own, :])
    scale = inverse_rms(x_own)
    small[0:1, 0:768] = jnp.sum(grad_nattn * x_own * scale, axis=0, keepdims=True)
    q = grad_nattn * gain_attn[...]
    inner = jnp.mean(q * x_own, axis=-1, keepdims=True)
    input_low[...] = (grad_mid[...] + scale * (q - x_own * scale * scale * inner)).astype(BF)

    @pl.when(second)
    def _():
        back_out.start()

    out_input[pl.ds(t * 128, 128), :] = input_low[...]
    input_gather = z_gather(own_order(out_input), own_order_far(out_input))
    input_gather.start()
    small_z[t] = small[:, 0:768]
    small_arrivals = [
        links.send(
            small.at[:, 0:768], small_z.at[t], ztx(k), small_z.at[(t + 4 - k) % 4]
        )
        for k in (1, 2, 3)
    ]
    attn_sum.pair_finish()
    ffn_sum.cross_start()

    def add_table(b, carry):
        hit = which == b
        for h in range(3):
            table_rows[h, pl.ds(b, 1), :] = jnp.sum(
                jnp.where(hit, bias[h], 0.0), axis=0, keepdims=True
            )
        return carry

    lax.fori_loop(0, 32, add_table, 0)
    ones = jnp.ones((8, 128), F32)
    for h in range(3):
        line = lax.dot_general(
            ones,
            table_rows[h],
            (((1,), (1,)), ((), ())),
            precision=lax.Precision.HIGHEST,
            preferred_element_type=F32,
        )
        small[h : h + 1, 768:896] = line[0:1, :]
    input_gather.forward()
    for arriving in small_arrivals:
        arriving.wait_recv()
    small_y[y, :, 0:768] = ((small_z[0] + small_z[1]) + small_z[2]) + small_z[3]
    small_y[y, :, 768:896] = small[:, 768:896]
    small_arrivals = [
        links.send(small_y.at[y], small_y.at[y], ydx(k), small_y.at[(y + 4 - k) % 4])
        for k in (1, 2, 3)
    ]
    attn_sum.relay()
    ffn_sum.cross_finish()
    for arriving in small_arrivals:
        arriving.wait_recv()
    place = 2 * xl + c
    small_xc[place] = ((small_y[0] + small_y[1]) + small_y[2]) + small_y[3]
    small_arrivals = [
        links.send(small_xc.at[place], small_xc.at[place], mate, small_xc.at[source])
        for mate, source in (
            (x_mate, 2 * (1 - xl) + c),
            (c_mate, 2 * xl + 1 - c),
            (xc_mate, 2 * (1 - xl) + 1 - c),
        )
    ]
    attn_sum.cross_start()
    ffn_sum.forward()
    attn_sum.cross_finish()
    for arriving in small_arrivals:
        arriving.wait_recv()
    total = ((small_xc[0] + small_xc[1]) + small_xc[2]) + small_xc[3]
    out_small[...] = total
    small_s[0] = total[:, 768:896]
    sections = links.send(small_s.at[0], small_s.at[1], s_mate)
    ffn_sum.share()
    attn_sum.forward()
    attn_sum.share()
    sections.wait_recv()
    out_small[:, 768:896] = small_s[0] + small_s[1]
    ffn_sum.finish()
    attn_sum.finish()
    hidden_gather.finish()
    input_gather.finish()

    @pl.when(second)
    def _():
        back_out.wait_send()

    links.drain()


def shards(
    embedded,
    expert_index,
    buckets,
    rel_bias,
    gain_attn,
    w_qkv,
    w_out,
    gain_ffn,
    w_router,
    w_in,
    w_down,
    cotangent,
):
    vmem, smem = pl.BlockSpec(memory_space=pltpu.VMEM), pl.BlockSpec(memory_space=pltpu.SMEM)
    hidden, grad_input, ffn, attn, small = pl.pallas_call(
        kernel,
        out_shape=[
            jax.ShapeDtypeStruct((512, 768), BF),
            jax.ShapeDtypeStruct((512, 768), BF),
            jax.ShapeDtypeStruct((3072, 768), BF),
            jax.ShapeDtypeStruct((768, 768), BF),
            jax.ShapeDtypeStruct((8, 896), F32),
        ],
        in_specs=[vmem, vmem, vmem, smem] + [vmem] * 8,
        out_specs=[vmem] * 5,
        scratch_shapes=[
            pltpu.VMEM((512, 768), BF),
            pltpu.VMEM((512, 768), BF),
            pltpu.VMEM((9, 512, 64), BF),
            pltpu.VMEM((12, 128, 128), F32),
            pltpu.VMEM((3, 128, 128), F32),
            pltpu.VMEM((4, 4, 128, 192), BF),
            pltpu.VMEM((4, 192, 768), BF),
            pltpu.VMEM((512, 768), F32),
            pltpu.VMEM((512, 768), BF),
            pltpu.VMEM((512, 1), F32),
            pltpu.VMEM((512, 1), F32),
            pltpu.VMEM((512, 768), BF),
            pltpu.VMEM((512, 768), F32),
            pltpu.VMEM((512, 768), BF),
            pltpu.VMEM((512, 768), BF),
            pltpu.VMEM((512, 768), BF),
            pltpu.VMEM((3, 6, 64, 768), BF),
            pltpu.VMEM((3, 2, 64, 768), BF),
            pltpu.VMEM((128, 768), F32),
            pltpu.VMEM((128, 768), BF),
            pltpu.VMEM((512, 768), BF),
            pltpu.VMEM((512, 768), BF),
            pltpu.VMEM((512, 768), BF),
            pltpu.VMEM((512, 768), BF),
            pltpu.VMEM((128, 768), F32),
            pltpu.VMEM((128, 768), BF),
            pltpu.VMEM((3, 512, 64), BF),
            pltpu.VMEM((512, 576), BF),
            pltpu.VMEM((3, 128, 128), F32),
            pltpu.VMEM((3072, 768), BF),
            pltpu.VMEM((768, 768), BF),
            pltpu.VMEM((1536, 768), BF),
            pltpu.VMEM((384, 768), BF),
            pltpu.VMEM((6, 192, 768), BF),
            pltpu.VMEM((6, 48, 768), BF),
            pltpu.VMEM((2, 192, 768), BF),
            pltpu.VMEM((2, 48, 768), BF),
            pltpu.VMEM((2, 384, 768), BF),
            pltpu.VMEM((2, 96, 768), BF),
            pltpu.VMEM((8, 896), F32),
            pltpu.VMEM((4, 8, 768), F32),
            pltpu.VMEM((4, 8, 896), F32),
            pltpu.VMEM((4, 8, 896), F32),
            pltpu.VMEM((2, 8, 128), F32),
            pltpu.SemaphoreType.DMA((COPIES,)),
            pltpu.SemaphoreType.DMA((COPIES,)),
        ],
        compiler_params=pltpu.CompilerParams(
            collective_id=0, has_side_effects=True, vmem_limit_bytes=60 * 1024 * 1024
        ),
    )(
        embedded,
        expert_index[0],
        buckets,
        rel_bias,
        gain_attn,
        w_qkv[0],
        w_out[0],
        gain_ffn,
        w_router[0].astype(F32).T,
        w_in[0],
        w_down[0],
        cotangent,
    )
    grad_qkv = jnp.transpose(attn[:576].reshape(3, 192, 768), (0, 2, 1)).astype(F32)
    ffn_wide = ffn.astype(F32)
    return (
        hidden.astype(F32)[None],
        grad_input.astype(F32)[None],
        small[0:3, 768:800].T,
        small[0:1, 0:768],
        grad_qkv[None],
        attn[576:].astype(F32)[None],
        small[1:2, 0:768],
        small[2:4, 0:768].T[None],
        ffn_wide[:1536].reshape(1, 2, 768, 768),
        ffn_wide[1536:].reshape(1, 2, 768, 768),
    )


def solution(mesh):
    in_specs = (
        P("dp", None),
        P("section", "dp", None),
        P(),
        P(None, "tensor"),
        P("section", None),
        P("section", None, None, "tensor"),
        P("section", "tensor", None),
        P("section", None),
        P("section", None, None),
        P("section", None, None, "tensor"),
        P("section", None, "tensor", None),
        P("dp", None),
    )
    out_specs = (
        P("section", "dp", None),
        P("section", "dp", None),
        P(None, "tensor"),
        P("section", None),
        P("section", None, None, "tensor"),
        P("section", "tensor", None),
        P("section", None),
        P("section", None, None),
        P("section", None, None, "tensor"),
        P("section", None, "tensor", None),
    )
    return jax.shard_map(shards, mesh=mesh, in_specs=in_specs, out_specs=out_specs, check_vma=False)
```

time: 910 us -> 233 us (0.26)
  waiting for transfers between devices: 572 us -> 0 us
  Pallas kernels: 0 us -> 211 us
  matrix products: 112 us -> 0 us
  other arithmetic: 68.3 us -> 6.22 us
  blocking collectives: 61.2 us -> 0 us
  local copies, waits for them, and re-layouts: 55.8 us -> 12.4 us
  between operations: 16.4 us -> 0.7 us
  starting transfers between devices: 14.1 us -> 0 us
    psum x13 -> x0, waiting for transfers between devices: 547 us -> none  [the longest x3 129 us: layer_forward(): lax.psum(partial_attn.astype(jnp.bfloat16), 'tensor').astype(jnp.float32)]
    pallas_call x0 -> x1, Pallas kernels: none -> 211 us  [shards(): pl.pallas_call(kernel, out_shape=[jax.ShapeDtypeStruct((512, 768), BF), j...]
    dot_general x64 -> x0, matrix products: 108 us -> none  [the longest x3 13.6 us: ffn_backward(): jnp.einsum('erf,erd->efd', activated.astype(jnp.bfloat16), grad_expert, p...]
    psum x2 -> x0, blocking collectives: 61.2 us -> none  [the longest x1 54.2 us: shards(): lax.psum(attn_totals[0].astype(jnp.bfloat16), 'dp').astype(jnp.float32)]
    unnamed x321 -> x12, local copies, waits for them, and re-layouts: 28.7 us -> 3.05 us
    ppermute x4 -> x0, waiting for transfers between devices: 24.4 us -> none  [from_behind(): return lax.ppermute(x, axis, pairs)]
    reduce_sum x29 -> x0, other arithmetic: 24.1 us -> none  [the longest x6 7.63 us: route_gate(): shifted = logits - jnp.max(logits, axis=-1, keepdims=True)]
    ppermute x4 -> x0, starting transfers between devices: 13.1 us -> none  [from_behind(): return lax.ppermute(x, axis, pairs)]
  transfers between devices with their start and end apart: 17 -> 0, of which waited for: 17 -> 0; matrix products, arithmetic and copies ran while one was open for 8% -> 0% of each run, Pallas kernels for 0% -> 0%
where the time goes in v1:
time: 233 us; the launch traced here: 231 us
  Pallas kernels  211 us (91%)
  local copies, waits for them, and re-layouts  12.4 us (5%)
  other arithmetic  6.22 us (3%)
    pallas_call x1, Pallas kernels, shards(): pl.pallas_call(kernel, out_shape=[jax.ShapeDtypeStruct((512, 768), BF), j...  211 us

profile of v1, /device:TPU:0, one launch (start us, length us, event | category | flops | bytes accessed | tf_op | source)
XLA Modules:
  0.0 230.8 jit_solution(3334917734572337794)
XLA Ops:
  0.6 0.0 copy-start.3
  0.7 0.0 copy-start.4
  0.7 0.0 copy-start.2
  0.7 2.3 %copy.24 = bf16[1,3,768,192]{3,2,1,0:T(8,128)(2,1)} copy(bf16[1,3,768,192]{2,3,1,0:T(8,128)(2,1)} %param.17) | data formatting | bytes 1769472 | tf_op args[5]
  3.0 0.0 copy-done.3
  3.0 0.9 copy.25.expert_index
  3.9 0.0 copy-done.4
  3.9 0.7 copy.26.rel_bias
  4.6 0.0 copy-done.2
  4.6 0.6 convert_bitcast_fusion.1.router
  5.2 211.5 %shard_map.195 = (bf16[512,768]{1,0:T(8,128)(2,1)}, bf16[512,768]{1,0:T(8,128)(2,1)}, bf16[3072,768]{1,0:T(8,128)(2,1)}, bf16[768,768]{1,0:T(8,128)(2,1)}, f32[8,896]{1,0:T(8,128)}) custom-call(bf16[512,768]{1,0:T(8,128)(2,1)} %embedded.1, s32[512,1]{1,0:T(8,128)} %copy.25.expert_index, s32[128,128]{1,0:T(8,128)} %buckets.1, f32[32,3]{1,0:T(8,128)} %copy.26.rel_bias, ...), custom_call_target="tpu_custom_call" | custom-call | tf_op jit(solution)/shard_map/pallas_call | solution.py:698
  216.7 0.0 copy-start
  216.7 3.4 %bitcast_convert_fusion = (f32[1,512,768]{2,1,0:T(8,128)}, f32[1,512,768]{2,1,0:T(8,128)}) fusion(bf16[512,768]{1,0:T(8,128)(2,1)} %get-tuple-element.16, bf16[512,768]{1,0:T(8,128)(2,1)} %get-tuple-element.15), kind=kLoop, calls=%fused_computation.1 | loop fusion | flops 786432 | bytes 4718592 | tf_op jit(solution)/shard_map/broadcast_in_dim | solution.py:778
  220.1 1.4 fusion.1
  221.5 1.3 slice_bitcast_fusion
  222.8 1.3 slice_bitcast_fusion.1
  224.1 0.0 copy-done
  224.1 0.0 copy-start.1
  224.1 4.5 %fusion = (f32[1536,768]{1,0:T(8,128)}, f32[1536,768]{1,0:T(8,128)}) fusion(bf16[3072,768]{1,0:T(8,128)(2,1)S(1)} %copy-done), kind=kLoop, calls=%fused_computation.7 | loop fusion | bytes 18874368 | tf_op jit(solution)/shard_map/slice | solution.py:786
  228.6 0.0 copy-done.1
  228.6 0.1 slice.26
  228.6 1.4 convert_bitcast_fusion
  230.0 0.9 bitcast_convert_fusion.2
Async XLA Ops:
  0.6 2.4 %copy-start.3 = (s32[1,512,1]{1,2,0:T(1,128)S(1)}, s32[1,512,1]{1,2,0:T(1,128)}, u32[]{:S(2)}) copy-start(s32[1,512,1]{1,2,0:T(1,128)} %param.13) | copy-start | bytes 6148
  0.7 3.2 %copy-start.4 = (f32[32,3]{0,1:T(4,128)S(1)}, f32[32,3]{0,1:T(4,128)}, u32[]{:S(2)}) copy-start(f32[32,3]{0,1:T(4,128)} %param.15) | copy-start | bytes 1156
  0.7 3.9 %copy-start.2 = (bf16[1,768,2]{1,2,0:T(2,128)(2,1)S(1)}, bf16[1,768,2]{1,2,0:T(2,128)(2,1)}, u32[]{:S(2)}) copy-start(bf16[1,768,2]{1,2,0:T(2,128)(2,1)} %param.20) | copy-start | bytes 9220
  216.7 7.4 %copy-start = (bf16[3072,768]{1,0:T(8,128)(2,1)S(1)}, bf16[3072,768]{1,0:T(8,128)(2,1)}, u32[]{:S(2)}) copy-start(bf16[3072,768]{1,0:T(8,128)(2,1)} %get-tuple-element.19) | copy-start | bytes 14155780
  224.1 4.5 %copy-start.1 = (bf16[768,768]{1,0:T(8,128)(2,1)S(1)}, bf16[768,768]{1,0:T(8,128)(2,1)}, u32[]{:S(2)}) copy-start(bf16[768,768]{1,0:T(8,128)(2,1)} %get-tuple-element.18) | copy-start | bytes 3538948
